TPU v7x, 512 devices: a whole 4x8x8 slice. The times are simulated.
512 devices in a mesh: blk: 32 (over z_hi, y, core), row: 16 (over x, z_lo).
Axes of the slice: x: 4, y: 8, z: 8 (z_hi: 2, z_lo: 4; z = z_hi * 4 + z_lo), core: 2. Of those that a mesh axis runs over, the one named last changes fastest.
Arguments:
- image: bfloat16 [49152, 1152], P(('blk', 'row')), may hold values from -0.1796875 to 0.1796875
- text: bfloat16 [49152, 1152], P(('blk', 'row')), may hold values from -0.1796875 to 0.1796875
- positive: int32 [49152], P(('blk', 'row')), may hold values from 0 to 1535
- plan: int32 [2, 32], replicated, may hold values from 0 to 31, as said below
- logit_scale: float32 [1], replicated, may hold values from 4 to 16
- logit_bias: float32 [1], replicated, may hold values from -4 to -1.5
Outputs:
- grad_image: bfloat16 [49152, 1152], P(('blk', 'row'))
- grad_text: bfloat16 [49152, 1152], P(('blk', 'row'))
Inputs may be any that keep to these rules, and one draw needn't show every extreme that they name: plan[k, i] = i XOR m_k, where the 2 masks m_k are distinct and nonzero.
All inputs are finite; a program needn't handle non-finite values.
Results may differ from a plain program's by a relative error of at most 0.025.
Values may be sent and summed in bfloat16 or wider, within the bound.
A program may use at most 64 MiB of HBM per device.

v0:
```python
import jax
import jax.numpy as jnp
from jax import lax
from jax.sharding import PartitionSpec as P


def swapped(value, axis, stride):
    mask = 2**stride
    pairs = [(source, source ^ mask) for source in range(lax.axis_size(axis))]
    return lax.ppermute(value, axis, pairs)


def unit_rows(x):
    xf = x.astype(jnp.float32)
    norm = jnp.sqrt(jnp.sum(xf * xf, axis=-1, keepdims=True) + 1e-06)
    return (xf / norm, norm)


def norm_backward(grad, unit, norm):
    return (grad - unit * jnp.sum(unit * grad, axis=-1, keepdims=True)) / norm


def logits(left, right, scale, bias):
    prod = lax.dot_general(
        left, right, (((1,), (1,)), ((), ())), preferred_element_type=jnp.float32
    )
    return scale * prod + bias


def select_bits(masks, level):
    return jnp.bitwise_and(jnp.right_shift(masks, level), 1) == 1


def fetch_partner(stack, masks):
    levels = lax.axis_size("blk").bit_length() - 1
    for level in range(levels):
        moved = swapped(stack, "blk", level)
        stack = jnp.where(select_bits(masks, level)[:, None, None], moved, stack)
    return stack


def return_partner(stack, masks):
    levels = lax.axis_size("blk").bit_length() - 1
    for level in range(levels):
        moved = swapped(stack, "blk", level)
        stack = jnp.where(select_bits(masks, level)[:, None, None], moved, stack)
    return stack


def shards(image, text, positive, plan, logit_scale, logit_bias):
    scale = logit_scale[0]
    bias = logit_bias[0]
    rows = image.shape[0]
    width = image.shape[1]
    img_unit, img_norm = unit_rows(image)
    txt_unit, txt_norm = unit_rows(text)
    img_hat = img_unit.astype(jnp.bfloat16)
    txt_hat = txt_unit.astype(jnp.bfloat16)
    text_block = lax.all_gather(txt_hat, "row", axis=0, tiled=True)
    columns = jnp.arange(text_block.shape[0], dtype=jnp.int32)
    labels = jnp.where(columns[None, :] == positive[:, None], 1.0, -1.0).astype(jnp.float32)
    self_scores = logits(img_hat, text_block, scale, bias)
    self_grad = (-labels * jax.nn.sigmoid(-labels * self_scores)).astype(jnp.bfloat16)
    img_grad = scale * jnp.dot(self_grad, text_block, preferred_element_type=jnp.float32)
    masks = plan[:, 0]
    rounds = plan.shape[0]
    lefts = [img_hat]
    grads = [self_grad]
    returned_list = []
    for step in range(rounds):
        partner_rows = fetch_partner(img_hat[None], masks[step : step + 1])
        count = partner_rows.shape[0]
        flat = partner_rows.reshape(count * rows, width)
        weights = jax.nn.sigmoid(logits(flat, text_block, scale, bias)).astype(jnp.bfloat16)
        back = (scale * jnp.dot(weights, text_block, preferred_element_type=jnp.float32)).astype(
            jnp.bfloat16
        )
        flat, weights, back = (flat, weights, back.reshape(count, rows, width))
        returned_list.append(return_partner(back, masks[step : step + 1]))
        lefts.append(flat)
        grads.append(weights)
    returned = jnp.concatenate(returned_list, axis=0)
    img_grad = img_grad + jnp.sum(returned.astype(jnp.float32), axis=0)
    left_all = jnp.concatenate(lefts, axis=0)
    grad_all = jnp.concatenate(grads, axis=0)
    partial_value = lax.dot_general(
        grad_all, left_all, (((0,), (0,)), ((), ())), preferred_element_type=jnp.float32
    )
    summed = lax.psum_scatter(
        partial_value.astype(jnp.bfloat16), "row", scatter_dimension=0, tiled=True
    ).astype(jnp.float32)
    txt_grad = scale * summed
    grad_image = norm_backward(img_grad, img_unit, img_norm).astype(jnp.bfloat16)
    grad_text = norm_backward(txt_grad, txt_unit, txt_norm).astype(jnp.bfloat16)
    return (grad_image, grad_text)


def solution(mesh):
    placed = (P(("blk", "row"), None), P(("blk", "row"), None), P(("blk", "row")), P(), P(), P())
    return jax.shard_map(
        shards,
        mesh=mesh,
        in_specs=placed,
        out_specs=(P(("blk", "row"), None), P(("blk", "row"), None)),
        check_vma=False,
    )
```

profile of v0, /device:TPU:24, one launch (start us, length us, event | category | flops | bytes accessed | tf_op | source)
XLA Modules:
  0.0 266.6 jit_solution(10271128165610644853)
XLA Ops:
  7.2 1.1 fusion.36
  8.3 1.7 fusion.39
  10.1 1.1 fusion.35
  11.2 1.1 fusion.53
  12.3 1.9 collective-permute-start
  14.2 1.4 fusion.40
  16.9 1.1 broadcast_select_fusion.10
  18.0 2.4 collective-permute-start.10
  20.4 1.7 fusion.38
  28.8 3.5 %collective-permute-start.1 = (bf16[1,96,1152]{2,1,0:T(8,128)(2,1)S(1)}, bf16[1,96,1152]{2,1,0:T(8,128)(2,1)S(1)}, u32[]{:S(2)}, u32[]{:S(2)}) collective-permute-start(bf16[1,96,1152]{2,1,0:T(8,128)(2,1)S(1)} %get-tuple-element.2), channel_id=1, source_target_pairs={{0,32},{16,48},{32,0},{48,16},{64,96},{80,112},{96,64},{112,80},{1... | collective-permute-start | bytes 663560 | tf_op jit(solution)/shard_map/ppermute | solution.py:10
  32.4 6.0 %collective-permute-start.11 = (bf16[1,96,1152]{2,1,0:T(8,128)(2,1)S(1)}, bf16[1,96,1152]{2,1,0:T(8,128)(2,1)S(1)}, u32[]{:S(2)}, u32[]{:S(2)}) collective-permute-start(bf16[1,96,1152]{2,1,0:T(8,128)(2,1)S(1)} %broadcast_select_fusion.3), channel_id=1, source_target_pairs={{0,64},{16,80},{32,96},{48,112},{64,0},{80,16},{96,32},{112,48},{1... | collective-permute-start | bytes 663560 | tf_op jit(solution)/shard_map/ppermute | solution.py:10
  38.5 8.2 %collective-permute-start.2 = (bf16[1,96,1152]{2,1,0:T(8,128)(2,1)S(1)}, bf16[1,96,1152]{2,1,0:T(8,128)(2,1)S(1)}, u32[]{:S(2)}, u32[]{:S(2)}) collective-permute-start(bf16[1,96,1152]{2,1,0:T(8,128)(2,1)S(1)} %broadcast_select_fusion.12), channel_id=1, source_target_pairs={{0,64},{16,80},{32,96},{48,112},{64,0},{80,16},{96,32},{112,48},{1... | collective-permute-start | bytes 663560 | tf_op jit(solution)/shard_map/ppermute | solution.py:10
  46.6 7.5 %collective-permute-done.11 = bf16[1,96,1152]{2,1,0:T(8,128)(2,1)S(1)} collective-permute-done((bf16[1,96,1152]{2,1,0:T(8,128)(2,1)S(1)}, bf16[1,96,1152]{2,1,0:T(8,128)(2,1)S(1)}, u32[]{:S(2)}, u32[]{:S(2)}) %collective-permute-start.11) | collective-permute-done | bytes 221216 | tf_op jit(solution)/shard_map/ppermute | solution.py:10
  54.1 3.9 %collective-permute-start.12 = (bf16[1,96,1152]{2,1,0:T(8,128)(2,1)S(1)}, bf16[1,96,1152]{2,1,0:T(8,128)(2,1)S(1)}, u32[]{:S(2)}, u32[]{:S(2)}) collective-permute-start(bf16[1,96,1152]{2,1,0:T(8,128)(2,1)S(1)} %broadcast_select_fusion.5), channel_id=1, source_target_pairs={{0,128},{16,144},{32,160},{48,176},{64,192},{80,208},{96,224},{112... | collective-permute-start | bytes 663560 | tf_op jit(solution)/shard_map/ppermute | solution.py:10
  58.6 5.4 %collective-permute-start.3 = (bf16[1,96,1152]{2,1,0:T(8,128)(2,1)S(1)}, bf16[1,96,1152]{2,1,0:T(8,128)(2,1)S(1)}, u32[]{:S(2)}, u32[]{:S(2)}) collective-permute-start(bf16[1,96,1152]{2,1,0:T(8,128)(2,1)S(1)} %broadcast_select_fusion.14), channel_id=1, source_target_pairs={{0,128},{16,144},{32,160},{48,176},{64,192},{80,208},{96,224},{112... | collective-permute-start | bytes 663560 | tf_op jit(solution)/shard_map/ppermute | solution.py:10
  63.9 10.9 %collective-permute-done.12 = bf16[1,96,1152]{2,1,0:T(8,128)(2,1)S(1)} collective-permute-done((bf16[1,96,1152]{2,1,0:T(8,128)(2,1)S(1)}, bf16[1,96,1152]{2,1,0:T(8,128)(2,1)S(1)}, u32[]{:S(2)}, u32[]{:S(2)}) %collective-permute-start.12) | collective-permute-done | bytes 221216 | tf_op jit(solution)/shard_map/ppermute | solution.py:10
  74.9 8.2 %collective-permute-start.13 = (bf16[1,96,1152]{2,1,0:T(8,128)(2,1)S(1)}, bf16[1,96,1152]{2,1,0:T(8,128)(2,1)S(1)}, u32[]{:S(2)}, u32[]{:S(2)}) collective-permute-start(bf16[1,96,1152]{2,1,0:T(8,128)(2,1)S(1)} %broadcast_select_fusion.7), channel_id=1, source_target_pairs={{0,256},{16,272},{32,288},{48,304},{64,320},{80,336},{96,352},{112... | collective-permute-start | bytes 663560 | tf_op jit(solution)/shard_map/ppermute | solution.py:10
  83.1 5.9 %collective-permute-start.4 = (bf16[1,96,1152]{2,1,0:T(8,128)(2,1)S(1)}, bf16[1,96,1152]{2,1,0:T(8,128)(2,1)S(1)}, u32[]{:S(2)}, u32[]{:S(2)}) collective-permute-start(bf16[1,96,1152]{2,1,0:T(8,128)(2,1)S(1)} %broadcast_select_fusion.16), channel_id=1, source_target_pairs={{0,256},{16,272},{32,288},{48,304},{64,320},{80,336},{96,352},{112... | collective-permute-start | bytes 663560 | tf_op jit(solution)/shard_map/ppermute | solution.py:10
  89.0 6.6 %collective-permute-done.13 = bf16[1,96,1152]{2,1,0:T(8,128)(2,1)S(1)} collective-permute-done((bf16[1,96,1152]{2,1,0:T(8,128)(2,1)S(1)}, bf16[1,96,1152]{2,1,0:T(8,128)(2,1)S(1)}, u32[]{:S(2)}, u32[]{:S(2)}) %collective-permute-start.13) | collective-permute-done | bytes 221216 | tf_op jit(solution)/shard_map/ppermute | solution.py:10
  96.4 9.7 %collective-permute-done.4 = bf16[1,96,1152]{2,1,0:T(8,128)(2,1)S(1)} collective-permute-done((bf16[1,96,1152]{2,1,0:T(8,128)(2,1)S(1)}, bf16[1,96,1152]{2,1,0:T(8,128)(2,1)S(1)}, u32[]{:S(2)}, u32[]{:S(2)}) %collective-permute-start.4) | collective-permute-done | bytes 221216 | tf_op jit(solution)/shard_map/ppermute | solution.py:10
  106.8 23.3 %all-gather.2.cloned.1.call-done = bf16[1536,1152]{1,0:T(8,128)(2,1)} async-done(((bf16[96,1152]{1,0:T(8,128)(2,1)}), bf16[1536,1152]{1,0:T(8,128)(2,1)}) %all-gather.2.cloned.1.call-update) | async-done | bytes 3538960 | tf_op jit(solution)/shard_map/all_gather | solution.py:59
  130.1 3.5 %fusion.18 = bf16[96,1536]{1,0:T(8,128)(2,1)S(1)} fusion(bf16[96,1152]{1,0:T(8,128)(2,1)} %select_bitcast_fusion, bf16[1536,1152]{1,0:T(8,128)(2,1)} %all-gather.2.cloned.1.call-done, f32[]{:T(128)} %bitcast.45, f32[]{:T(128)} %bitcast.38), kind=kOutput, calls=%fused_computation.25 | convolution fusion | flops 340623360 | bytes 4055048 | tf_op jit(solution)/shard_map/dot_general | solution.py:24
  133.7 1.2 fusion.19
  135.0 1.3 fusion.20
  137.0 3.9 %convolution_convert_fusion = bf16[1536,1152]{1,0:T(8,128)(2,1)} fusion(bf16[96,1536]{1,0:T(8,128)(2,1)S(1)} %fusion.18, bf16[96,1536]{1,0:T(8,128)(2,1)S(1)} %fusion.19, bf16[96,1536]{1,0:T(8,128)(2,1)S(1)} %fusion.20, bf16[96,1152]{1,0:T(8,128)(2,1)S(1)} %copy-done.5, bf16[96,1152]{1,0:T(8,128)(2,1)S(1)} %copy-done.6, bf16[96,1152]{1,0:T(8,128)(2,1)S(1)} %copy-done.7), kind=kOutput, calls=%fused_computation | convolution fusion | flops 1025630208 | bytes 5087232 | tf_op jit(solution)/shard_map/dot_general | solution.py:86
  141.0 1.7 fusion.23
  142.7 1.9 collective-permute-start.14
  145.4 2.4 collective-permute-start.5
  147.9 2.8 %collective-permute-start.15 = (bf16[1,96,1152]{2,1,0:T(8,128)(2,1)S(1)}, bf16[1,96,1152]{2,1,0:T(8,128)(2,1)S(1)}, u32[]{:S(2)}, u32[]{:S(2)}) collective-permute-start(bf16[1,96,1152]{2,1,0:T(8,128)(2,1)S(1)} %broadcast_select_fusion), channel_id=1, source_target_pairs={{0,32},{16,48},{32,0},{48,16},{64,96},{80,112},{96,64},{112,80},{1... | collective-permute-start | bytes 663560 | tf_op jit(solution)/shard_map/ppermute | solution.py:10
  150.7 3.2 %collective-permute-start.6 = (bf16[1,96,1152]{2,1,0:T(8,128)(2,1)S(1)}, bf16[1,96,1152]{2,1,0:T(8,128)(2,1)S(1)}, u32[]{:S(2)}, u32[]{:S(2)}) collective-permute-start(bf16[1,96,1152]{2,1,0:T(8,128)(2,1)S(1)} %broadcast_select_fusion.9), channel_id=1, source_target_pairs={{0,32},{16,48},{32,0},{48,16},{64,96},{80,112},{96,64},{112,80},{1... | collective-permute-start | bytes 663560 | tf_op jit(solution)/shard_map/ppermute | solution.py:10
  153.9 4.3 %collective-permute-done.15 = bf16[1,96,1152]{2,1,0:T(8,128)(2,1)S(1)} collective-permute-done((bf16[1,96,1152]{2,1,0:T(8,128)(2,1)S(1)}, bf16[1,96,1152]{2,1,0:T(8,128)(2,1)S(1)}, u32[]{:S(2)}, u32[]{:S(2)}) %collective-permute-start.15) | collective-permute-done | bytes 221216 | tf_op jit(solution)/shard_map/ppermute | solution.py:10
  158.2 2.4 collective-permute-start.16
  160.6 1.4 collective-permute-done.6
  162.0 3.0 %collective-permute-start.7 = (bf16[1,96,1152]{2,1,0:T(8,128)(2,1)S(1)}, bf16[1,96,1152]{2,1,0:T(8,128)(2,1)S(1)}, u32[]{:S(2)}, u32[]{:S(2)}) collective-permute-start(bf16[1,96,1152]{2,1,0:T(8,128)(2,1)S(1)} %broadcast_select_fusion.11), channel_id=1, source_target_pairs={{0,64},{16,80},{32,96},{48,112},{64,0},{80,16},{96,32},{112,48},{1... | collective-permute-start | bytes 663560 | tf_op jit(solution)/shard_map/ppermute | solution.py:10
  165.0 11.4 %collective-permute-done.16 = bf16[1,96,1152]{2,1,0:T(8,128)(2,1)S(1)} collective-permute-done((bf16[1,96,1152]{2,1,0:T(8,128)(2,1)S(1)}, bf16[1,96,1152]{2,1,0:T(8,128)(2,1)S(1)}, u32[]{:S(2)}, u32[]{:S(2)}) %collective-permute-start.16) | collective-permute-done | bytes 221216 | tf_op jit(solution)/shard_map/ppermute | solution.py:10
  176.4 5.9 %collective-permute-start.17 = (bf16[1,96,1152]{2,1,0:T(8,128)(2,1)S(1)}, bf16[1,96,1152]{2,1,0:T(8,128)(2,1)S(1)}, u32[]{:S(2)}, u32[]{:S(2)}) collective-permute-start(bf16[1,96,1152]{2,1,0:T(8,128)(2,1)S(1)} %broadcast_select_fusion.4), channel_id=1, source_target_pairs={{0,128},{16,144},{32,160},{48,176},{64,192},{80,208},{96,224},{112... | collective-permute-start | bytes 663560 | tf_op jit(solution)/shard_map/ppermute | solution.py:10
  182.4 3.9 %collective-permute-start.8 = (bf16[1,96,1152]{2,1,0:T(8,128)(2,1)S(1)}, bf16[1,96,1152]{2,1,0:T(8,128)(2,1)S(1)}, u32[]{:S(2)}, u32[]{:S(2)}) collective-permute-start(bf16[1,96,1152]{2,1,0:T(8,128)(2,1)S(1)} %broadcast_select_fusion.13), channel_id=1, source_target_pairs={{0,128},{16,144},{32,160},{48,176},{64,192},{80,208},{96,224},{112... | collective-permute-start | bytes 663560 | tf_op jit(solution)/shard_map/ppermute | solution.py:10
  186.3 10.2 %collective-permute-done.17 = bf16[1,96,1152]{2,1,0:T(8,128)(2,1)S(1)} collective-permute-done((bf16[1,96,1152]{2,1,0:T(8,128)(2,1)S(1)}, bf16[1,96,1152]{2,1,0:T(8,128)(2,1)S(1)}, u32[]{:S(2)}, u32[]{:S(2)}) %collective-permute-start.17) | collective-permute-done | bytes 221216 | tf_op jit(solution)/shard_map/ppermute | solution.py:10
  196.5 2.3 collective-permute-start.18
  198.8 3.4 %collective-permute-done.8 = bf16[1,96,1152]{2,1,0:T(8,128)(2,1)S(1)} collective-permute-done((bf16[1,96,1152]{2,1,0:T(8,128)(2,1)S(1)}, bf16[1,96,1152]{2,1,0:T(8,128)(2,1)S(1)}, u32[]{:S(2)}, u32[]{:S(2)}) %collective-permute-start.8) | collective-permute-done | bytes 221216 | tf_op jit(solution)/shard_map/ppermute | solution.py:10
  202.2 5.9 %collective-permute-start.9 = (bf16[1,96,1152]{2,1,0:T(8,128)(2,1)S(1)}, bf16[1,96,1152]{2,1,0:T(8,128)(2,1)S(1)}, u32[]{:S(2)}, u32[]{:S(2)}) collective-permute-start(bf16[1,96,1152]{2,1,0:T(8,128)(2,1)S(1)} %broadcast_select_fusion.15), channel_id=1, source_target_pairs={{0,256},{16,272},{32,288},{48,304},{64,320},{80,336},{96,352},{112... | collective-permute-start | bytes 663560 | tf_op jit(solution)/shard_map/ppermute | solution.py:10
  208.1 10.0 %collective-permute-done.18 = bf16[1,96,1152]{2,1,0:T(8,128)(2,1)S(1)} collective-permute-done((bf16[1,96,1152]{2,1,0:T(8,128)(2,1)S(1)}, bf16[1,96,1152]{2,1,0:T(8,128)(2,1)S(1)}, u32[]{:S(2)}, u32[]{:S(2)}) %collective-permute-start.18) | collective-permute-done | bytes 221216 | tf_op jit(solution)/shard_map/ppermute | solution.py:10
  218.1 11.5 %collective-permute-done.9 = bf16[1,96,1152]{2,1,0:T(8,128)(2,1)S(1)} collective-permute-done((bf16[1,96,1152]{2,1,0:T(8,128)(2,1)S(1)}, bf16[1,96,1152]{2,1,0:T(8,128)(2,1)S(1)}, u32[]{:S(2)}, u32[]{:S(2)}) %collective-permute-start.9) | collective-permute-done | bytes 221216 | tf_op jit(solution)/shard_map/ppermute | solution.py:10
  229.7 0.8 multiply_reduce_fusion.1
  230.5 0.9 divide_convert_fusion.1
  231.4 25.2 %reduce-scatter.2.cloned.1.call-done = bf16[96,1152]{1,0:T(8,128)(2,1)} async-done(((bf16[1536,1152]{1,0:T(8,128)(2,1)}), bf16[96,1152]{1,0:T(8,128)(2,1)}) %reduce-scatter.2.cloned.1.call-update) | async-done | bytes 221200 | tf_op jit(solution)/shard_map/reduce_scatter | solution.py:89
  256.5 1.3 multiply_reduce_fusion
  257.8 1.9 divide_convert_fusion
  (56 shorter events, 4.1 us)
Async XLA Ops:
  7.2 123.0 %all-gather.2.cloned.1.call-start = ((), (), s32[]{:S(2)}) async-start(), calls=%async_computation.1 | async-start | bytes 3760128 | tf_op jit(solution)/shard_map/all_gather | solution.py:59
  10.1 246.5 %reduce-scatter.2.cloned.1.call-start = ((), (), s32[]{:S(2)}) async-start(), calls=%async_computation.2 | async-start | bytes 3760128 | tf_op jit(solution)/shard_map/reduce_scatter | solution.py:89
  12.3 4.6 %collective-permute-start = (bf16[1,96,1152]{2,1,0:T(8,128)(2,1)S(1)}, bf16[1,96,1152]{2,1,0:T(8,128)(2,1)S(1)}, u32[]{:S(2)}, u32[]{:S(2)}) collective-permute-start(bf16[1,96,1152]{2,1,0:T(8,128)(2,1)S(1)} %fusion.53), channel_id=1, source_target_pairs={{0,16},{16,0},{32,48},{48,32},{64,80},{80,64},{96,112},{112,96},{1... | collective-permute-start | bytes 663560 | tf_op jit(solution)/shard_map/ppermute | solution.py:10
  18.0 14.3 %collective-permute-start.10 = (bf16[1,96,1152]{2,1,0:T(8,128)(2,1)S(1)}, bf16[1,96,1152]{2,1,0:T(8,128)(2,1)S(1)}, u32[]{:S(2)}, u32[]{:S(2)}) collective-permute-start(bf16[1,96,1152]{2,1,0:T(8,128)(2,1)S(1)} %get-tuple-element.3), channel_id=1, source_target_pairs={{0,32},{16,48},{32,0},{48,16},{64,96},{80,112},{96,64},{112,80},{1... | collective-permute-start | bytes 663560 | tf_op jit(solution)/shard_map/ppermute | solution.py:10
  28.8 9.6 %collective-permute-start.1 = (bf16[1,96,1152]{2,1,0:T(8,128)(2,1)S(1)}, bf16[1,96,1152]{2,1,0:T(8,128)(2,1)S(1)}, u32[]{:S(2)}, u32[]{:S(2)}) collective-permute-start(bf16[1,96,1152]{2,1,0:T(8,128)(2,1)S(1)} %get-tuple-element.2), channel_id=1, source_target_pairs={{0,32},{16,48},{32,0},{48,16},{64,96},{80,112},{96,64},{112,80},{1... | collective-permute-start | bytes 663560 | tf_op jit(solution)/shard_map/ppermute | solution.py:10
  32.4 21.7 %collective-permute-start.11 = (bf16[1,96,1152]{2,1,0:T(8,128)(2,1)S(1)}, bf16[1,96,1152]{2,1,0:T(8,128)(2,1)S(1)}, u32[]{:S(2)}, u32[]{:S(2)}) collective-permute-start(bf16[1,96,1152]{2,1,0:T(8,128)(2,1)S(1)} %broadcast_select_fusion.3), channel_id=1, source_target_pairs={{0,64},{16,80},{32,96},{48,112},{64,0},{80,16},{96,32},{112,48},{1... | collective-permute-start | bytes 663560 | tf_op jit(solution)/shard_map/ppermute | solution.py:10
  38.5 20.1 %collective-permute-start.2 = (bf16[1,96,1152]{2,1,0:T(8,128)(2,1)S(1)}, bf16[1,96,1152]{2,1,0:T(8,128)(2,1)S(1)}, u32[]{:S(2)}, u32[]{:S(2)}) collective-permute-start(bf16[1,96,1152]{2,1,0:T(8,128)(2,1)S(1)} %broadcast_select_fusion.12), channel_id=1, source_target_pairs={{0,64},{16,80},{32,96},{48,112},{64,0},{80,16},{96,32},{112,48},{1... | collective-permute-start | bytes 663560 | tf_op jit(solution)/shard_map/ppermute | solution.py:10
  54.1 20.7 %collective-permute-start.12 = (bf16[1,96,1152]{2,1,0:T(8,128)(2,1)S(1)}, bf16[1,96,1152]{2,1,0:T(8,128)(2,1)S(1)}, u32[]{:S(2)}, u32[]{:S(2)}) collective-permute-start(bf16[1,96,1152]{2,1,0:T(8,128)(2,1)S(1)} %broadcast_select_fusion.5), channel_id=1, source_target_pairs={{0,128},{16,144},{32,160},{48,176},{64,192},{80,208},{96,224},{112... | collective-permute-start | bytes 663560 | tf_op jit(solution)/shard_map/ppermute | solution.py:10
  58.6 24.5 %collective-permute-start.3 = (bf16[1,96,1152]{2,1,0:T(8,128)(2,1)S(1)}, bf16[1,96,1152]{2,1,0:T(8,128)(2,1)S(1)}, u32[]{:S(2)}, u32[]{:S(2)}) collective-permute-start(bf16[1,96,1152]{2,1,0:T(8,128)(2,1)S(1)} %broadcast_select_fusion.14), channel_id=1, source_target_pairs={{0,128},{16,144},{32,160},{48,176},{64,192},{80,208},{96,224},{112... | collective-permute-start | bytes 663560 | tf_op jit(solution)/shard_map/ppermute | solution.py:10
  74.9 20.8 %collective-permute-start.13 = (bf16[1,96,1152]{2,1,0:T(8,128)(2,1)S(1)}, bf16[1,96,1152]{2,1,0:T(8,128)(2,1)S(1)}, u32[]{:S(2)}, u32[]{:S(2)}) collective-permute-start(bf16[1,96,1152]{2,1,0:T(8,128)(2,1)S(1)} %broadcast_select_fusion.7), channel_id=1, source_target_pairs={{0,256},{16,272},{32,288},{48,304},{64,320},{80,336},{96,352},{112... | collective-permute-start | bytes 663560 | tf_op jit(solution)/shard_map/ppermute | solution.py:10
  83.1 23.0 %collective-permute-start.4 = (bf16[1,96,1152]{2,1,0:T(8,128)(2,1)S(1)}, bf16[1,96,1152]{2,1,0:T(8,128)(2,1)S(1)}, u32[]{:S(2)}, u32[]{:S(2)}) collective-permute-start(bf16[1,96,1152]{2,1,0:T(8,128)(2,1)S(1)} %broadcast_select_fusion.16), channel_id=1, source_target_pairs={{0,256},{16,272},{32,288},{48,304},{64,320},{80,336},{96,352},{112... | collective-permute-start | bytes 663560 | tf_op jit(solution)/shard_map/ppermute | solution.py:10
  130.1 3.5 %copy-start = (bf16[1536,1152]{1,0:T(8,128)(2,1)S(1)}, bf16[1536,1152]{1,0:T(8,128)(2,1)}, u32[]{:S(2)}) copy-start(bf16[1536,1152]{1,0:T(8,128)(2,1)} %all-gather.2.cloned.1.call-done) | copy-start | bytes 10616836
  130.1 3.5 %copy-start.6 = (bf16[96,1152]{1,0:T(8,128)(2,1)S(1)}, bf16[96,1152]{1,0:T(8,128)(2,1)}, u32[]{:S(2)}) copy-start(bf16[96,1152]{1,0:T(8,128)(2,1)} %select_bitcast_fusion.1) | copy-start | bytes 663556
  133.6 2.6 copy-start.4
  133.6 1.3 copy-start.7
  133.6 1.3 copy-start.8
  134.9 1.3 copy-start.2
  134.9 2.1 copy-start.5
  136.3 0.7 copy-start.9
  141.0 3.7 %copy-start.3 = (bf16[96,1536]{1,0:T(8,128)(2,1)S(1)}, bf16[96,1536]{1,0:T(8,128)(2,1)}, u32[]{:S(2)}) copy-start(bf16[96,1536]{1,0:T(8,128)(2,1)} %copy-done.2) | copy-start | bytes 884740
  142.7 5.1 %collective-permute-start.14 = (bf16[1,96,1152]{2,1,0:T(8,128)(2,1)S(1)}, bf16[1,96,1152]{2,1,0:T(8,128)(2,1)S(1)}, u32[]{:S(2)}, u32[]{:S(2)}) collective-permute-start(bf16[1,96,1152]{2,1,0:T(8,128)(2,1)S(1)} %fusion.23), channel_id=1, source_target_pairs={{0,16},{16,0},{32,48},{48,32},{64,80},{80,64},{96,112},{112,96},{1... | collective-permute-start | bytes 663560 | tf_op jit(solution)/shard_map/ppermute | solution.py:10
  145.4 5.3 %collective-permute-start.5 = (bf16[1,96,1152]{2,1,0:T(8,128)(2,1)S(1)}, bf16[1,96,1152]{2,1,0:T(8,128)(2,1)S(1)}, u32[]{:S(2)}, u32[]{:S(2)}) collective-permute-start(bf16[1,96,1152]{2,1,0:T(8,128)(2,1)S(1)} %fusion.24), channel_id=1, source_target_pairs={{0,16},{16,0},{32,48},{48,32},{64,80},{80,64},{96,112},{112,96},{1... | collective-permute-start | bytes 663560 | tf_op jit(solution)/shard_map/ppermute | solution.py:10
  147.8 81.8 %copy-start.1 = (bf16[96,1152]{1,0:T(8,128)(2,1)S(1)}, bf16[96,1152]{1,0:T(8,128)(2,1)}, u32[]{:S(2)}) copy-start(bf16[96,1152]{1,0:T(8,128)(2,1)} %param.6) | copy-start | bytes 663556
  147.9 81.8 %copy-start.10 = (bf16[96,1536]{1,0:T(8,128)(2,1)S(1)}, bf16[96,1536]{1,0:T(8,128)(2,1)}, u32[]{:S(2)}) copy-start(bf16[96,1536]{1,0:T(8,128)(2,1)} %copy-done.9) | copy-start | bytes 884740
  147.9 10.3 %collective-permute-start.15 = (bf16[1,96,1152]{2,1,0:T(8,128)(2,1)S(1)}, bf16[1,96,1152]{2,1,0:T(8,128)(2,1)S(1)}, u32[]{:S(2)}, u32[]{:S(2)}) collective-permute-start(bf16[1,96,1152]{2,1,0:T(8,128)(2,1)S(1)} %broadcast_select_fusion), channel_id=1, source_target_pairs={{0,32},{16,48},{32,0},{48,16},{64,96},{80,112},{96,64},{112,80},{1... | collective-permute-start | bytes 663560 | tf_op jit(solution)/shard_map/ppermute | solution.py:10
  150.7 11.3 %collective-permute-start.6 = (bf16[1,96,1152]{2,1,0:T(8,128)(2,1)S(1)}, bf16[1,96,1152]{2,1,0:T(8,128)(2,1)S(1)}, u32[]{:S(2)}, u32[]{:S(2)}) collective-permute-start(bf16[1,96,1152]{2,1,0:T(8,128)(2,1)S(1)} %broadcast_select_fusion.9), channel_id=1, source_target_pairs={{0,32},{16,48},{32,0},{48,16},{64,96},{80,112},{96,64},{112,80},{1... | collective-permute-start | bytes 663560 | tf_op jit(solution)/shard_map/ppermute | solution.py:10
  158.2 18.2 %collective-permute-start.16 = (bf16[1,96,1152]{2,1,0:T(8,128)(2,1)S(1)}, bf16[1,96,1152]{2,1,0:T(8,128)(2,1)S(1)}, u32[]{:S(2)}, u32[]{:S(2)}) collective-permute-start(bf16[1,96,1152]{2,1,0:T(8,128)(2,1)S(1)} %broadcast_select_fusion.2), channel_id=1, source_target_pairs={{0,64},{16,80},{32,96},{48,112},{64,0},{80,16},{96,32},{112,48},{1... | collective-permute-start | bytes 663560 | tf_op jit(solution)/shard_map/ppermute | solution.py:10
  162.0 20.3 %collective-permute-start.7 = (bf16[1,96,1152]{2,1,0:T(8,128)(2,1)S(1)}, bf16[1,96,1152]{2,1,0:T(8,128)(2,1)S(1)}, u32[]{:S(2)}, u32[]{:S(2)}) collective-permute-start(bf16[1,96,1152]{2,1,0:T(8,128)(2,1)S(1)} %broadcast_select_fusion.11), channel_id=1, source_target_pairs={{0,64},{16,80},{32,96},{48,112},{64,0},{80,16},{96,32},{112,48},{1... | collective-permute-start | bytes 663560 | tf_op jit(solution)/shard_map/ppermute | solution.py:10
  176.4 20.0 %collective-permute-start.17 = (bf16[1,96,1152]{2,1,0:T(8,128)(2,1)S(1)}, bf16[1,96,1152]{2,1,0:T(8,128)(2,1)S(1)}, u32[]{:S(2)}, u32[]{:S(2)}) collective-permute-start(bf16[1,96,1152]{2,1,0:T(8,128)(2,1)S(1)} %broadcast_select_fusion.4), channel_id=1, source_target_pairs={{0,128},{16,144},{32,160},{48,176},{64,192},{80,208},{96,224},{112... | collective-permute-start | bytes 663560 | tf_op jit(solution)/shard_map/ppermute | solution.py:10
  182.4 19.8 %collective-permute-start.8 = (bf16[1,96,1152]{2,1,0:T(8,128)(2,1)S(1)}, bf16[1,96,1152]{2,1,0:T(8,128)(2,1)S(1)}, u32[]{:S(2)}, u32[]{:S(2)}) collective-permute-start(bf16[1,96,1152]{2,1,0:T(8,128)(2,1)S(1)} %broadcast_select_fusion.13), channel_id=1, source_target_pairs={{0,128},{16,144},{32,160},{48,176},{64,192},{80,208},{96,224},{112... | collective-permute-start | bytes 663560 | tf_op jit(solution)/shard_map/ppermute | solution.py:10
  196.5 21.6 %collective-permute-start.18 = (bf16[1,96,1152]{2,1,0:T(8,128)(2,1)S(1)}, bf16[1,96,1152]{2,1,0:T(8,128)(2,1)S(1)}, u32[]{:S(2)}, u32[]{:S(2)}) collective-permute-start(bf16[1,96,1152]{2,1,0:T(8,128)(2,1)S(1)} %broadcast_select_fusion.6), channel_id=1, source_target_pairs={{0,256},{16,272},{32,288},{48,304},{64,320},{80,336},{96,352},{112... | collective-permute-start | bytes 663560 | tf_op jit(solution)/shard_map/ppermute | solution.py:10
  202.2 27.4 %collective-permute-start.9 = (bf16[1,96,1152]{2,1,0:T(8,128)(2,1)S(1)}, bf16[1,96,1152]{2,1,0:T(8,128)(2,1)S(1)}, u32[]{:S(2)}, u32[]{:S(2)}) collective-permute-start(bf16[1,96,1152]{2,1,0:T(8,128)(2,1)S(1)} %broadcast_select_fusion.15), channel_id=1, source_target_pairs={{0,256},{16,272},{32,288},{48,304},{64,320},{80,336},{96,352},{112... | collective-permute-start | bytes 663560 | tf_op jit(solution)/shard_map/ppermute | solution.py:10
Sparse Core Ops, SparseCore 0:
  10.7 119.4 all-gather.1
  141.1 115.3 reduce-scatter.1
where the time goes:
time: 268 us; the launch traced here: 267 us
  waiting for transfers between devices  136 us (51%)
  starting transfers between devices  79 us (29%)
  between operations  22.5 us (8%)
  other arithmetic  13.9 us (5%)
  matrix products  13.2 us (5%)
    ppermute x19, waiting for transfers between devices, swapped(): return lax.ppermute(value, axis, pairs)  87.3 us
    ppermute x19, starting transfers between devices, swapped(): return lax.ppermute(value, axis, pairs)  78.9 us
    reduce_scatter x1, waiting for transfers between devices, shards(): lax.psum_scatter(partial_value.astype(jnp.bfloat16), 'row', scatter_dimen...  25.2 us
    all_gather x1, waiting for transfers between devices, shards(): text_block = lax.all_gather(txt_hat, 'row', axis=0, tiled=True)  23.3 us
    dot_general x3, matrix products, logits(): lax.dot_general(left, right, (((1,), (1,)), ((), ())), preferred_element_...  6.02 us
  transfers between devices with their start and end apart: 21, of which 14 were waited for; matrix products, arithmetic and copies ran while one was open for 5% of the time, Pallas kernels for 0%

commit v1 on v0

--- a/solution.py
+++ b/solution.py
@@ -4,10 +4,14 @@
 from jax.sharding import PartitionSpec as P
 
 
-def swapped(value, axis, stride):
-    mask = 2**stride
-    pairs = [(source, source ^ mask) for source in range(lax.axis_size(axis))]
-    return lax.ppermute(value, axis, pairs)
+def exchange(value, mask):
+    count = lax.axis_size("blk")
+
+    def branch(m):
+        pairs = [(source, source ^ m) for source in range(count)]
+        return lambda v: lax.ppermute(v, "blk", pairs)
+
+    return lax.switch(mask - 1, [branch(m) for m in range(1, count)], value)
 
 
 def unit_rows(x):
@@ -27,31 +31,9 @@
     return scale * prod + bias
 
 
-def select_bits(masks, level):
-    return jnp.bitwise_and(jnp.right_shift(masks, level), 1) == 1
-
-
-def fetch_partner(stack, masks):
-    levels = lax.axis_size("blk").bit_length() - 1
-    for level in range(levels):
-        moved = swapped(stack, "blk", level)
-        stack = jnp.where(select_bits(masks, level)[:, None, None], moved, stack)
-    return stack
-
-
-def return_partner(stack, masks):
-    levels = lax.axis_size("blk").bit_length() - 1
-    for level in range(levels):
-        moved = swapped(stack, "blk", level)
-        stack = jnp.where(select_bits(masks, level)[:, None, None], moved, stack)
-    return stack
-
-
 def shards(image, text, positive, plan, logit_scale, logit_bias):
     scale = logit_scale[0]
     bias = logit_bias[0]
-    rows = image.shape[0]
-    width = image.shape[1]
     img_unit, img_norm = unit_rows(image)
     txt_unit, txt_norm = unit_rows(text)
     img_hat = img_unit.astype(jnp.bfloat16)
@@ -68,19 +50,16 @@
     grads = [self_grad]
     returned_list = []
     for step in range(rounds):
-        partner_rows = fetch_partner(img_hat[None], masks[step : step + 1])
-        count = partner_rows.shape[0]
-        flat = partner_rows.reshape(count * rows, width)
+        flat = exchange(img_hat, masks[step])
         weights = jax.nn.sigmoid(logits(flat, text_block, scale, bias)).astype(jnp.bfloat16)
         back = (scale * jnp.dot(weights, text_block, preferred_element_type=jnp.float32)).astype(
             jnp.bfloat16
         )
-        flat, weights, back = (flat, weights, back.reshape(count, rows, width))
-        returned_list.append(return_partner(back, masks[step : step + 1]))
+        returned_list.append(exchange(back, masks[step]))
         lefts.append(flat)
         grads.append(weights)
-    returned = jnp.concatenate(returned_list, axis=0)
-    img_grad = img_grad + jnp.sum(returned.astype(jnp.float32), axis=0)
+    for term in returned_list:
+        img_grad = img_grad + term.astype(jnp.float32)
     left_all = jnp.concatenate(lefts, axis=0)
     grad_all = jnp.concatenate(grads, axis=0)
     partial_value = lax.dot_general(

time: 268 us -> 236 us (0.88)
  the two profiles are of different devices: /device:TPU:24 before, /device:TPU:8 now
where the time goes in v1:
time: 236 us; the launch traced here: 235 us
  waiting for transfers between devices  173 us (73%)
  matrix products  18.7 us (8%)
  between operations  16.7 us (7%)
  starting transfers between devices  14.6 us (6%)
  other arithmetic  9.67 us (4%)
    all_gather x1, waiting for transfers between devices, shards(): text_block = lax.all_gather(txt_hat, 'row', axis=0, tiled=True)  60.4 us
    reduce_scatter x1, waiting for transfers between devices, shards(): lax.psum_scatter(partial_value.astype(jnp.bfloat16), 'row', scatter_dimen...  58.5 us
    ppermute x4, waiting for transfers between devices, branch(): return lambda v: lax.ppermute(v, 'blk', pairs)  54.3 us
    ppermute x4, starting transfers between devices, branch(): return lambda v: lax.ppermute(v, 'blk', pairs)  14.5 us
    dot_general x3, matrix products, logits(): lax.dot_general(left, right, (((1,), (1,)), ((), ())), preferred_element_...  8.07 us
    dot_general x1, matrix products, shards(): lax.dot_general(grad_all, left_all, (((0,), (0,)), ((), ())), preferred_e...  5.13 us
  transfers between devices with their start and end apart: 6, of which 6 were waited for; matrix products, arithmetic and copies ran while one was open for 4% of the time, Pallas kernels for 0%

profile of v1, /device:TPU:8, one launch (start us, length us, event | category | flops | bytes accessed | tf_op | source)
XLA Modules:
  0.0 234.9 jit_solution(5957345936040464837)
XLA Ops:
  7.2 0.0 all-gather.2.cloned.1.call-start
  7.2 1.1 fusion.35
  8.3 1.7 fusion.38
  10.1 0.0 all-gather.2.cloned.1.call-update
  10.1 0.0 reduce-scatter.2.cloned.1.call-start
  11.4 1.3 fusion.39
  13.9 1.1 fusion.34
  15.0 1.7 fusion.37
  16.8 18.6 %conditional.12 = (bf16[96,1152]{1,0:T(8,128)(2,1)}) conditional(s32[]{:T(128)} %bitcast.3, bf16[96,1152]{1,0:T(8,128)(2,1)} %fusion.37, bf16[96,1152]{1,0:T(8,128)(2,1)} %fusion.37, bf16[96,1152]{1,0:T(8,128)(2,1)} %fusion.37, bf16[96,1152]{1,0:T(8,128)(2,1)} %fusion.37, bf16[96,1152]{1,0:T(8,128)(2,1)} %fusion.37, ...), branch_computations={%region_64.65_spmd, %region_65.66_spmd, %region_66.67_spmd, %regio... | conditional | bytes 884784 | solution.py:14
  16.8 6.3 %collective-permute-start.70 = (bf16[96,1152]{1,0:T(8,128)(2,1)}, bf16[96,1152]{1,0:T(8,128)(2,1)}, u32[]{:S(2)}, u32[]{:S(2)}) collective-permute-start(bf16[96,1152]{1,0:T(8,128)(2,1)} %param.70), channel_id=1, source_target_pairs={{0,144},{16,128},{32,176},{48,160},{64,208},{80,192},{96,240},{112... | collective-permute-start | bytes 663560 | tf_op jit(solution)/shard_map/cond/branch_8_fun/ppermute | solution.py:12
  23.0 12.3 %collective-permute-done.70 = bf16[96,1152]{1,0:T(8,128)(2,1)} collective-permute-done((bf16[96,1152]{1,0:T(8,128)(2,1)}, bf16[96,1152]{1,0:T(8,128)(2,1)}, u32[]{:S(2)}, u32[]{:S(2)}) %collective-permute-start.70) | collective-permute-done | bytes 221216 | tf_op jit(solution)/shard_map/cond/branch_8_fun/ppermute | solution.py:12
  35.3 17.6 %conditional.10 = (bf16[96,1152]{1,0:T(8,128)(2,1)}) conditional(s32[]{:T(128)} %bitcast.2, bf16[96,1152]{1,0:T(8,128)(2,1)} %fusion.37, bf16[96,1152]{1,0:T(8,128)(2,1)} %fusion.37, bf16[96,1152]{1,0:T(8,128)(2,1)} %fusion.37, bf16[96,1152]{1,0:T(8,128)(2,1)} %fusion.37, bf16[96,1152]{1,0:T(8,128)(2,1)} %fusion.37, ...), branch_computations={%region_2.3_spmd, %region_3.4_spmd, %region_4.5_spmd, %region_5.6_... | conditional | bytes 884784 | solution.py:14
  35.3 4.4 %collective-permute-start.10 = (bf16[96,1152]{1,0:T(8,128)(2,1)}, bf16[96,1152]{1,0:T(8,128)(2,1)}, u32[]{:S(2)}, u32[]{:S(2)}) collective-permute-start(bf16[96,1152]{1,0:T(8,128)(2,1)} %param.10), channel_id=1, source_target_pairs={{0,176},{16,160},{32,144},{48,128},{64,240},{80,224},{96,208},{112... | collective-permute-start | bytes 663560 | tf_op jit(solution)/shard_map/cond/branch_10_fun/ppermute | solution.py:12
  39.7 13.2 %collective-permute-done.10 = bf16[96,1152]{1,0:T(8,128)(2,1)} collective-permute-done((bf16[96,1152]{1,0:T(8,128)(2,1)}, bf16[96,1152]{1,0:T(8,128)(2,1)}, u32[]{:S(2)}, u32[]{:S(2)}) %collective-permute-start.10) | collective-permute-done | bytes 221216 | tf_op jit(solution)/shard_map/cond/branch_10_fun/ppermute | solution.py:12
  52.9 60.4 %all-gather.2.cloned.1.call-done = bf16[1536,1152]{1,0:T(8,128)(2,1)} async-done(((bf16[96,1152]{1,0:T(8,128)(2,1)}), bf16[1536,1152]{1,0:T(8,128)(2,1)}) %all-gather.2.cloned.1.call-update) | async-done | bytes 3538960 | tf_op jit(solution)/shard_map/all_gather | solution.py:41
  113.3 0.0 copy-start
  113.3 3.5 %fusion.19 = bf16[96,1536]{1,0:T(8,128)(2,1)S(1)} fusion(bf16[96,1152]{1,0:T(8,128)(2,1)} %get-tuple-element.272, bf16[1536,1152]{1,0:T(8,128)(2,1)} %all-gather.2.cloned.1.call-done, f32[]{:T(128)} %bitcast.25, f32[]{:T(128)} %bitcast.18), kind=kOutput, calls=%fused_computation.26 | convolution fusion | flops 340623360 | bytes 4055048 | tf_op jit(solution)/shard_map/dot_general | solution.py:28
  116.8 0.0 copy-start.3
  116.8 0.0 copy-start.4
  116.8 0.0 copy-done
  116.8 2.3 fusion.20
  119.1 0.0 copy-start.2
  119.1 0.0 copy-done.4
  119.1 2.3 fusion.21
  121.4 0.0 copy-done.3
  121.4 0.0 copy-done.2
  121.4 0.0 copy-start.5
  121.4 0.7 copy-done.5
  122.1 5.1 %convolution_convert_fusion = bf16[1536,1152]{1,0:T(8,128)(2,1)} fusion(bf16[96,1536]{1,0:T(8,128)(2,1)S(1)} %fusion.19, bf16[96,1536]{1,0:T(8,128)(2,1)S(1)} %fusion.20, bf16[96,1536]{1,0:T(8,128)(2,1)S(1)} %fusion.21, bf16[96,1152]{1,0:T(8,128)(2,1)} %get-tuple-element.272, bf16[96,1152]{1,0:T(8,128)(2,1)} %get-tuple-element.270, bf16[96,1152]{1,0:T(8,128)(2,1)} %fusion.37), kind=kOutput, calls=%fused_computation | convolution fusion | flops 1025630208 | bytes 5087232 | tf_op jit(solution)/shard_map/dot_general | solution.py:65
  127.3 0.0 reduce-scatter.2.cloned.1.call-update
  127.3 1.7 fusion.23
  129.0 17.4 %conditional.13 = (bf16[96,1152]{1,0:T(8,128)(2,1)}) conditional(s32[]{:T(128)} %bitcast.3, bf16[96,1152]{1,0:T(8,128)(2,1)S(1)} %fusion.23, bf16[96,1152]{1,0:T(8,128)(2,1)S(1)} %fusion.23, bf16[96,1152]{1,0:T(8,128)(2,1)S(1)} %fusion.23, bf16[96,1152]{1,0:T(8,128)(2,1)S(1)} %fusion.23, ...), branch_computations={%region_95.96_spmd, %region_96.97_spmd, %region_97.98_spmd, %regio... | conditional | bytes 884784
  129.0 1.9 collective-permute-start.101
  130.9 15.5 %collective-permute-done.101 = bf16[96,1152]{1,0:T(8,128)(2,1)} collective-permute-done((bf16[96,1152]{1,0:T(8,128)(2,1)S(1)}, bf16[96,1152]{1,0:T(8,128)(2,1)}, u32[]{:S(2)}, u32[]{:S(2)}) %collective-permute-start.101) | collective-permute-done | bytes 221216 | tf_op jit(solution)/shard_map/cond/branch_8_fun/ppermute | solution.py:12
  146.4 1.7 fusion.22
  148.1 15.3 %conditional.11 = (bf16[96,1152]{1,0:T(8,128)(2,1)}) conditional(s32[]{:T(128)} %bitcast.2, bf16[96,1152]{1,0:T(8,128)(2,1)S(1)} %fusion.22, bf16[96,1152]{1,0:T(8,128)(2,1)S(1)} %fusion.22, bf16[96,1152]{1,0:T(8,128)(2,1)S(1)} %fusion.22, bf16[96,1152]{1,0:T(8,128)(2,1)S(1)} %fusion.22, ...), branch_computations={%region_33.34_spmd, %region_34.35_spmd, %region_35.36_spmd, %regio... | conditional | bytes 884784
  148.1 1.9 collective-permute-start.41
  150.1 13.4 %collective-permute-done.41 = bf16[96,1152]{1,0:T(8,128)(2,1)} collective-permute-done((bf16[96,1152]{1,0:T(8,128)(2,1)S(1)}, bf16[96,1152]{1,0:T(8,128)(2,1)}, u32[]{:S(2)}, u32[]{:S(2)}) %collective-permute-start.41) | collective-permute-done | bytes 221216 | tf_op jit(solution)/shard_map/cond/branch_10_fun/ppermute | solution.py:12
  163.4 0.0 copy-start.1
  163.4 2.1 multiply_reduce_fusion.1
  165.6 0.0 copy-done.1
  165.6 0.8 divide_convert_fusion.1
  166.4 58.5 %reduce-scatter.2.cloned.1.call-done = bf16[96,1152]{1,0:T(8,128)(2,1)} async-done(((bf16[1536,1152]{1,0:T(8,128)(2,1)}), bf16[96,1152]{1,0:T(8,128)(2,1)}) %reduce-scatter.2.cloned.1.call-update) | async-done | bytes 221200 | tf_op jit(solution)/shard_map/reduce_scatter | solution.py:68
  224.9 1.3 multiply_reduce_fusion
  226.2 1.9 divide_convert_fusion
  (2 shorter events, 0.0 us)
Async XLA Ops:
  7.2 106.1 %all-gather.2.cloned.1.call-start = ((), (), s32[]{:S(2)}) async-start(), calls=%async_computation.1 | async-start | bytes 3760128 | tf_op jit(solution)/shard_map/all_gather | solution.py:41
  10.1 214.8 %reduce-scatter.2.cloned.1.call-start = ((), (), s32[]{:S(2)}) async-start(), calls=%async_computation.2 | async-start | bytes 3760128 | tf_op jit(solution)/shard_map/reduce_scatter | solution.py:68
  16.8 18.6 %collective-permute-start.70 = (bf16[96,1152]{1,0:T(8,128)(2,1)}, bf16[96,1152]{1,0:T(8,128)(2,1)}, u32[]{:S(2)}, u32[]{:S(2)}) collective-permute-start(bf16[96,1152]{1,0:T(8,128)(2,1)} %param.70), channel_id=1, source_target_pairs={{0,144},{16,128},{32,176},{48,160},{64,208},{80,192},{96,240},{112... | collective-permute-start | bytes 663560 | tf_op jit(solution)/shard_map/cond/branch_8_fun/ppermute | solution.py:12
  35.3 17.6 %collective-permute-start.10 = (bf16[96,1152]{1,0:T(8,128)(2,1)}, bf16[96,1152]{1,0:T(8,128)(2,1)}, u32[]{:S(2)}, u32[]{:S(2)}) collective-permute-start(bf16[96,1152]{1,0:T(8,128)(2,1)} %param.10), channel_id=1, source_target_pairs={{0,176},{16,160},{32,144},{48,128},{64,240},{80,224},{96,208},{112... | collective-permute-start | bytes 663560 | tf_op jit(solution)/shard_map/cond/branch_10_fun/ppermute | solution.py:12
  113.3 3.5 %copy-start = (bf16[1536,1152]{1,0:T(8,128)(2,1)S(1)}, bf16[1536,1152]{1,0:T(8,128)(2,1)}, u32[]{:S(2)}) copy-start(bf16[1536,1152]{1,0:T(8,128)(2,1)} %all-gather.2.cloned.1.call-done) | copy-start | bytes 10616836
  116.8 4.6 %copy-start.3 = (bf16[96,1536]{1,0:T(8,128)(2,1)}, bf16[96,1536]{1,0:T(8,128)(2,1)S(1)}, u32[]{:S(2)}) copy-start(bf16[96,1536]{1,0:T(8,128)(2,1)S(1)} %fusion.19) | copy-start | bytes 884740
  116.8 2.3 copy-start.4
  119.1 2.3 copy-start.2
  121.4 0.7 copy-start.5
  129.0 17.4 %collective-permute-start.101 = (bf16[96,1152]{1,0:T(8,128)(2,1)S(1)}, bf16[96,1152]{1,0:T(8,128)(2,1)}, u32[]{:S(2)}, u32[]{:S(2)}) collective-permute-start(bf16[96,1152]{1,0:T(8,128)(2,1)S(1)} %param.101), channel_id=1, source_target_pairs={{0,144},{16,128},{32,176},{48,160},{64,208},{80,192},{96,240},{112... | collective-permute-start | bytes 663560 | tf_op jit(solution)/shard_map/cond/branch_8_fun/ppermute | solution.py:12
  148.1 15.3 %collective-permute-start.41 = (bf16[96,1152]{1,0:T(8,128)(2,1)S(1)}, bf16[96,1152]{1,0:T(8,128)(2,1)}, u32[]{:S(2)}, u32[]{:S(2)}) collective-permute-start(bf16[96,1152]{1,0:T(8,128)(2,1)S(1)} %param.41), channel_id=1, source_target_pairs={{0,176},{16,160},{32,144},{48,128},{64,240},{80,224},{96,208},{112... | collective-permute-start | bytes 663560 | tf_op jit(solution)/shard_map/cond/branch_10_fun/ppermute | solution.py:12
  163.4 2.1 copy-start.1
Sparse Core Ops, SparseCore 0:
  10.7 102.5 all-gather.1
  127.4 97.4 reduce-scatter.1
